TPU v7x, 32 devices: a whole 2x2x4 slice. The times are simulated.
32 devices in a mesh: dp: 8 (over y, x, core), tensor: 4 (over z).
Axes of the slice: x: 2, y: 2, z: 4, core: 2. Of those that a mesh axis runs over, the one named last changes fastest.
Arguments:
- hidden_states: bfloat16 [6144, 4096], P('dp', 'tensor')
- neighbour_ids: int32 [96, 2], P('dp'), may hold values from 0 to 127, as said below
- database: bfloat16 [128, 128, 896], P('dp')
- w_up: bfloat16 [896, 3584], P(None, 'tensor'), may hold values from -0.1875 to 0.1875
- w_down: bfloat16 [3584, 896], P('tensor'), may hold values from -0.09375 to 0.09375
- w_query: bfloat16 [4096, 4096], P(None, 'tensor'), may hold values from -0.09375 to 0.09375
- w_key: bfloat16 [896, 4096], P(None, 'tensor'), may hold values from -0.1875 to 0.1875
- w_value: bfloat16 [896, 4096], P(None, 'tensor'), may hold values from -0.1875 to 0.1875
Outputs:
- attended: bfloat16 [6144, 4096], P('dp', 'tensor')
Inputs may be any that keep to these rules, and one draw needn't show every extreme that they name: `neighbour_ids`: block ids are grouped by owner: index s of dp holds blocks s * 16 to (s + 1) * 16 - 1. Among the 24 ids of one sequence, no owner's blocks are named more than 4 times; one owner, the same for every sequence, is named exactly 4 times by each.
All inputs are finite; a program needn't handle non-finite values.
Results may differ from a plain program's by a relative error of at most 0.02.
Values may be sent and summed in bfloat16 or wider, within the bound.
A program may use at most 128 MiB of HBM per device.

v0:
```python
import math

import jax
import jax.numpy as jnp
from jax import lax
from jax.sharding import PartitionSpec as P

HD = 128
SPAN = 64
KN = 2
NTOK = 128


EPSILON = 1e-06
LOGIT_SCALE = 3.0


def head_norm(projected):
    shaped = projected.reshape(projected.shape[0], -1, HD)
    scaled = shaped * lax.rsqrt(jnp.mean(shaped * shaped, axis=-1, keepdims=True) + EPSILON)
    return scaled.astype(jnp.bfloat16)


def attend(queries, keys, values):
    seq_rows = queries.shape[0]
    heads_here = queries.shape[1]
    span_count = seq_rows // SPAN
    shifted = jnp.concatenate(
        [queries[SPAN - 1 :], jnp.zeros((SPAN - 1, heads_here, HD), jnp.bfloat16)], axis=0
    )
    windows = shifted.reshape(span_count, SPAN, heads_here, HD)
    key_blocks = keys.reshape(span_count, KN * NTOK, heads_here, HD)
    value_blocks = values.reshape(span_count, KN * NTOK, heads_here, HD)
    scores = jnp.einsum("cqhd,ckhd->chqk", windows, key_blocks, preferred_element_type=jnp.float32)
    scores = scores * (LOGIT_SCALE / math.sqrt(HD))
    expo = jnp.exp(scores)
    weights = (expo / jnp.sum(expo, axis=-1, keepdims=True)).astype(jnp.bfloat16)
    mixed = jnp.einsum("chqk,ckhd->cqhd", weights, value_blocks, preferred_element_type=jnp.float32)
    mixed = mixed.astype(jnp.bfloat16).reshape(seq_rows, heads_here * HD)
    leading = jnp.zeros((SPAN - 1, heads_here * HD), jnp.bfloat16)
    return jnp.concatenate([leading, mixed[: seq_rows - SPAN + 1]], axis=0)


def shards(hidden_states, neighbour_ids, database, w_up, w_down, w_query, w_key, w_value):
    dp_count = lax.axis_size("dp")
    tensor_count = lax.axis_size("tensor")
    shard_blocks = database.shape[0]
    block_tokens = database.shape[1]
    enc_width = database.shape[2]
    flat_ids = neighbour_ids.reshape(-1)
    request_count = flat_ids.shape[0]
    capacity = max(2, (request_count + dp_count - 1) // dp_count + 1)
    owners = flat_ids // shard_blocks
    local_rows = flat_ids % shard_blocks
    owner_match = (owners[:, None] == jnp.arange(dp_count, dtype=jnp.int32)[None, :]).astype(
        jnp.int32
    )
    positions = jnp.arange(request_count, dtype=jnp.int32)
    earlier = (positions[:, None] > positions[None, :]).astype(jnp.int32)
    ranks = jnp.sum(jnp.dot(earlier, owner_match) * owner_match, axis=1)
    slots = owners * capacity + ranks
    slot_match = slots[None, :] == jnp.arange(dp_count * capacity, dtype=jnp.int32)[:, None]
    requests = jnp.sum(jnp.where(slot_match, local_rows[None, :], 0), axis=1)
    requests = requests.reshape(dp_count, capacity)
    replies = lax.all_to_all(
        database[lax.all_to_all(requests, "dp", split_axis=0, concat_axis=0, tiled=True)],
        "dp",
        split_axis=0,
        concat_axis=0,
        tiled=True,
    )
    raw_blocks = replies.reshape(dp_count * capacity, block_tokens, enc_width)[slots]
    raw_float = raw_blocks.astype(jnp.float32)
    normed = (
        raw_float * lax.rsqrt(jnp.mean(raw_float * raw_float, axis=-1, keepdims=True) + EPSILON)
    ).astype(jnp.bfloat16)
    own_blocks = request_count // tensor_count
    inner = jnp.einsum("bte,ef->btf", normed, w_up, preferred_element_type=jnp.float32)
    active = jax.nn.gelu(inner).astype(jnp.bfloat16)
    summed = lax.psum_scatter(
        jnp.einsum("btf,fe->bte", active, w_down, preferred_element_type=jnp.float32).astype(
            jnp.bfloat16
        ),
        "tensor",
        scatter_dimension=0,
        tiled=True,
    ).astype(jnp.float32)
    raw_own = lax.dynamic_slice_in_dim(
        raw_float, lax.axis_index("tensor") * own_blocks, own_blocks, 0
    )
    encoded_own = (raw_own + summed).astype(jnp.bfloat16)
    encoded = lax.all_gather(encoded_own, "tensor", axis=0, tiled=True)
    projected = jnp.dot(
        lax.all_gather(hidden_states, "tensor", axis=1, tiled=True),
        w_query,
        preferred_element_type=jnp.float32,
    )
    queries = head_norm(projected)
    flat_encoded = encoded.reshape(-1, enc_width)
    keys = head_norm(jnp.dot(flat_encoded, w_key, preferred_element_type=jnp.float32))
    values = jnp.dot(flat_encoded, w_value, preferred_element_type=jnp.float32).astype(jnp.bfloat16)
    values = values.reshape(flat_encoded.shape[0], -1, HD)
    return attend(queries, keys, values)


def solution(mesh):
    in_specs = (
        P("dp", "tensor"),
        P("dp", None),
        P("dp", None, None),
        P(None, "tensor"),
        P("tensor", None),
        P(None, "tensor"),
        P(None, "tensor"),
        P(None, "tensor"),
    )
    out_specs = P("dp", "tensor")
    return jax.shard_map(shards, mesh=mesh, in_specs=in_specs, out_specs=out_specs, check_vma=False)
```

profile of v0, /device:TPU:0, one launch (start us, length us, event | category | flops | bytes accessed | tf_op | source)
XLA Modules:
  0.0 503.6 jit_solution(10944675326901660564)
XLA Ops:
  6.5 0.9 copy.56
  7.4 0.1 reshape.233
  7.5 0.1 fusion.38
  7.7 0.1 select_reduce_fusion
  7.8 0.1 all_to_all.11
  7.9 9.6 %all_to_all.17 = s32[8,1,4]{2,1,0:T(1,128)S(1)} all-to-all(s32[8,1,4]{2,1,0:T(1,128)S(1)} %bitcast.57), channel_id=1, replica_groups=mesh['dp'=8,'tensor'=4] {'dp'}, dimensions={0} | all-to-all | bytes 256 | tf_op jit(solution)/shard_map/all_to_all | solution.py:66
  17.5 0.1 copy.58
  17.6 0.1 copy.59
  17.7 0.1 reshape.243
  17.8 6.5 %gather_fusion = bf16[32,128,896]{2,1,0:T(8,128)(2,1)} fusion(bf16[16,128,896]{2,1,0:T(8,128)(2,1)} %param.10, s32[1024]{0:T(1024)S(1)} %pad_clamp_fusion.1), kind=kCustom, calls=%fused_computation | custom fusion | bytes 14680192 | tf_op jit(solution)/shard_map/gather | solution.py:66
  24.2 4.8 all-to-all-start.1
  29.1 0.0 reduce-scatter.2.cloned.1.call-start
  29.1 0.1 reshape.235
  29.2 82.7 %all-to-all-done.1 = bf16[8,4,128,896]{3,2,1,0:T(8,128)(2,1)} async-done(((bf16[8,4,128,896]{3,2,1,0:T(8,128)(2,1)}), bf16[8,4,128,896]{3,2,1,0:T(8,128)(2,1)}, u32[]{:S(2)}, u32[]{:S(2)}) %all-to-all-start.1) | async-done | bytes 7340064 | tf_op jit(solution)/shard_map/all_to_all | solution.py:65
  111.9 7.0 %gather_fusion.1 = bf16[24,128,896]{2,1,0:T(8,128)(2,1)} fusion(bf16[32,128,896]{2,1,0:T(8,128)(2,1)} %bitcast.3, s32[1024]{0:T(1024)S(1)} %pad_clamp_fusion), kind=kCustom, calls=%fused_computation.1 | custom fusion | bytes 11010144 | tf_op jit(solution)/shard_map/gather | solution.py:72
  118.9 3.8 multiply_reduce_fusion.1
  122.7 18.1 %fusion.22 = bf16[24,128,896]{2,1,0:T(8,128)(2,1)} fusion(f32[24,128]{1,0:T(8,128)S(1)} %add_rsqrt_fusion.2, bf16[24,128,896]{2,1,0:T(8,128)(2,1)} %gather_fusion.1, bf16[896,896]{1,0:T(8,128)(2,1)S(1)} %copy-done.4, bf16[896,896]{1,0:T(8,128)(2,1)} %param.11), kind=kOutput, calls=%fused_computation.31 | convolution fusion | flops 9900785664 | bytes 14233600 | tf_op jit(solution)/shard_map/btf,fe->bte/dot_general | solution.py:81
  140.9 0.0 reduce-scatter.2.cloned.1.call-update
  140.9 0.0 all-gather.5.cloned.1.call-start
  141.0 0.7 all-gather.5.cloned.1.call-update
  141.7 0.0 all-gather.3.cloned.1.call-start
  141.7 8.5 %convert_element_type.38 = f32[24,128,896]{2,1,0:T(8,128)} convert(bf16[24,128,896]{2,1,0:T(8,128)(2,1)} %gather_fusion.1) | non-fusion elementwise | flops 2752512 | bytes 16515072 | tf_op jit(solution)/shard_map/convert_element_type | solution.py:73
  150.2 88.3 %reduce-scatter.2.cloned.1.call-done = bf16[6,128,896]{2,1,0:T(8,128)(2,1)} async-done(((bf16[24,128,896]{2,1,0:T(8,128)(2,1)}), bf16[6,128,896]{2,1,0:T(8,128)(2,1)}) %reduce-scatter.2.cloned.1.call-update) | async-done | bytes 1376272 | tf_op jit(solution)/shard_map/reduce_scatter | solution.py:80
  238.5 3.6 add_convert_fusion
  242.0 0.0 all-gather.3.cloned.1.call-update
  242.1 4.0 copy.68
  246.1 109.9 %all-gather.5.cloned.1.call-done = bf16[768,4096]{1,0:T(8,128)(2,1)} async-done(((bf16[768,1024]{1,0:T(8,128)(2,1)}), bf16[768,4096]{1,0:T(8,128)(2,1)}) %all-gather.5.cloned.1.call-update) | async-done | bytes 6291472 | tf_op jit(solution)/shard_map/all_gather | solution.py:94
  355.9 10.9 %convolution_bitcast_fusion = f32[96,8,8,128]{3,1,2,0:T(8,128)S(1)} fusion(bf16[768,4096]{1,0:T(8,128)(2,1)} %all-gather.5.cloned.1.call-done, bf16[4096,1024]{1,0:T(8,128)(2,1)} %param.13), kind=kOutput, calls=%fused_computation.38 | convolution fusion | flops 6442450944 | bytes 17825792 | tf_op jit(solution)/shard_map/dot_general | solution.py:93
  366.8 0.7 copy.69
  367.6 1.6 copy-done.1
  369.2 0.9 multiply_reduce_fusion.2
  370.1 0.1 copy.61
  370.3 0.1 slice.13
  370.3 0.2 copy.83
  370.5 3.0 fusion.27
  373.5 0.1 concatenate.6
  373.7 84.4 %all-gather.3.cloned.1.call-done = bf16[24,128,896]{2,1,0:T(8,128)(2,1)} async-done(((bf16[6,128,896]{2,1,0:T(8,128)(2,1)}), bf16[24,128,896]{2,1,0:T(8,128)(2,1)}) %all-gather.3.cloned.1.call-update) | async-done | bytes 5505040 | tf_op jit(solution)/shard_map/all_gather | solution.py:92
  458.1 10.6 %multiply_reduce_fusion = (f32[3072,8]{0,1:T(8,128)S(1)}, f32[3072,8,128]{2,0,1:T(8,128)S(1)}) fusion(bf16[3072,896,1]{1,0,2:T(8,128)(2,1)} %bitcast.58, bf16[8,128,896]{2,1,0:T(8,128)(2,1)} %bitcast.56), kind=kOutput, calls=%fused_computation.4 | convolution fusion | flops 5643411456 | bytes 20021248 | tf_op jit(solution)/shard_map/dot_general | solution.py:100
  468.8 8.7 %convert_bitcast_fusion = bf16[384,8,8,128]{3,1,2,0:T(8,128)(2,1)} fusion(bf16[3072,896]{1,0:T(8,128)(2,1)S(1)} %bitcast.59, bf16[896,1024]{1,0:T(8,128)(2,1)S(1)} %copy-done), kind=kOutput, calls=%fused_computation.21 | convolution fusion | flops 5640290304 | bytes 13631488 | tf_op jit(solution)/shard_map/dot_general | solution.py:101
  477.5 7.1 %copy.70 = bf16[384,8,8,128]{3,2,1,0:T(8,128)(2,1)} copy(bf16[384,8,8,128]{3,1,2,0:T(8,128)(2,1)} %convert_bitcast_fusion) | data formatting | bytes 12582912
  484.6 3.8 multiply_convert_fusion
  488.5 2.4 fusion.12
  490.9 0.4 copy-done.2
  491.2 2.5 fusion.35
  493.7 1.2 copy.67
  494.9 0.4 copy.88
  495.4 0.1 slice.14
  495.5 1.5 concatenate.7
  (17 shorter events, 0.1 us)
Async XLA Ops:
  6.5 462.2 %copy-start = (bf16[896,1024]{1,0:T(8,128)(2,1)S(1)}, bf16[896,1024]{1,0:T(8,128)(2,1)}, u32[]{:S(2)}) copy-start(bf16[896,1024]{1,0:T(8,128)(2,1)} %param.15) | copy-start | bytes 5505028
  24.2 87.7 %all-to-all-start.1 = ((bf16[8,4,128,896]{3,2,1,0:T(8,128)(2,1)}), bf16[8,4,128,896]{3,2,1,0:T(8,128)(2,1)}, u32[]{:S(2)}, u32[]{:S(2)}) async-start(bf16[8,4,128,896]{3,2,1,0:T(8,128)(2,1)} %bitcast.47), calls=%async_computation.1 | async-start | bytes 14680064 | tf_op jit(solution)/shard_map/all_to_all | solution.py:65
  29.1 209.4 %reduce-scatter.2.cloned.1.call-start = ((), (), s32[]{:S(2)}) async-start(), calls=%async_computation.3 | async-start | bytes 6881280 | tf_op jit(solution)/shard_map/reduce_scatter | solution.py:80
  118.9 3.8 copy-start.4
  140.9 215.0 %all-gather.5.cloned.1.call-start = ((), (), s32[]{:S(2)}) async-start(), calls=%async_computation.5 | async-start | bytes 7864320 | tf_op jit(solution)/shard_map/all_gather | solution.py:94
  141.7 316.4 %all-gather.3.cloned.1.call-start = ((), (), s32[]{:S(2)}) async-start(), calls=%async_computation.4 | async-start | bytes 6881280 | tf_op jit(solution)/shard_map/all_gather | solution.py:92
  367.6 1.7 copy-start.1
  458.1 10.7 %copy-start.3 = (bf16[24,128,896]{2,1,0:T(8,128)(2,1)S(1)}, bf16[24,128,896]{2,1,0:T(8,128)(2,1)}, u32[]{:S(2)}) copy-start(bf16[24,128,896]{2,1,0:T(8,128)(2,1)} %all-gather.3.cloned.1.call-done) | copy-start | bytes 16515076
  488.4 2.8 copy-start.2
Sparse Core Ops, SparseCore 0:
  141.0 97.3 reduce-scatter.1
  240.0 115.8 all-gather.4
  357.5 100.5 all-gather.2
where the time goes:
time: 504 us
  waiting for transfers between devices  366 us (73%)
  matrix products  53.4 us (11%)
  local copies, waits for them, and re-layouts  32.5 us (6%)
  other arithmetic  23.8 us (5%)
  between operations  13.3 us (3%)
  blocking collectives  9.63 us (2%)
    all_gather x1, waiting for transfers between devices, shards(): lax.all_gather(hidden_states, 'tensor', axis=1, tiled=True)  110 us
    reduce_scatter x1, waiting for transfers between devices, shards(): lax.psum_scatter(jnp.einsum('btf,fe->bte', active, w_down, preferred_elem...  88.3 us
    all_gather x1, waiting for transfers between devices, shards(): encoded = lax.all_gather(encoded_own, 'tensor', axis=0, tiled=True)  84.4 us
    all_to_all x1, waiting for transfers between devices, shards(): lax.all_to_all(database[lax.all_to_all(requests, 'dp', split_axis=0, conc...  82.7 us
    dot_general x1, matrix products, shards(): jnp.einsum('btf,fe->bte', active, w_down, preferred_element_type=jnp.floa...  18.1 us
    unnamed x15, local copies, waits for them, and re-layouts  11.3 us
    dot_general x1, matrix products, shards(): jnp.dot(lax.all_gather(hidden_states, 'tensor', axis=1, tiled=True), w_qu...  10.9 us
    dot_general x1, matrix products, shards(): jnp.dot(flat_encoded, w_key, preferred_element_type=jnp.float32)  10.6 us
  transfers between devices with their start and end apart: 4, of which 4 were waited for; matrix products, arithmetic and copies ran while one was open for 6% of the time, Pallas kernels for 0%

commit v1 on v0

v1 whole, which is shorter than its diff:
```python
import functools
import math

import jax
import jax.numpy as jnp
from jax import lax
from jax.experimental import pallas as pl
from jax.experimental.pallas import tpu as pltpu
from jax.sharding import PartitionSpec as P

HD = 128
SPAN = 64
KN = 2
NTOK = 128

EPSILON = 1e-06
LOGIT_SCALE = 3.0
PARTS = 2
GROUP = 4
MIB = 1024 * 1024


def pick_kernel(parts, ids_ref, block_ref, *out_refs):
    rows = block_ref.shape[1] // parts
    for part in range(parts):
        out_refs[part][...] = block_ref[:, part * rows : (part + 1) * rows, :]


def pick_blocks(ids, database, parts):
    count = ids.shape[0]
    _, tokens, width = database.shape
    rows = tokens // parts
    return pl.pallas_call(
        functools.partial(pick_kernel, parts),
        grid_spec=pltpu.PrefetchScalarGridSpec(
            num_scalar_prefetch=1,
            grid=(count,),
            in_specs=[pl.BlockSpec((1, tokens, width), lambda i, ids_ref: (ids_ref[i], 0, 0))],
            out_specs=[pl.BlockSpec((1, rows, width), lambda i, ids_ref: (i, 0, 0))] * parts,
        ),
        out_shape=[jax.ShapeDtypeStruct((count, rows, width), database.dtype)] * parts,
        cost_estimate=pl.CostEstimate(
            flops=0, bytes_accessed=4 * count * tokens * width, transcendentals=0
        ),
    )(ids, database)


def encode_kernel(slots_ref, *refs):
    blocks = refs[:GROUP]
    up_ref, down_ref, key_ref, value_ref, keys_ref, values_ref = refs[GROUP:]
    raw = jnp.concatenate([ref[0] for ref in blocks], axis=0).astype(jnp.float32)
    normed = (
        raw * lax.rsqrt(jnp.mean(raw * raw, axis=-1, keepdims=True) + EPSILON)
    ).astype(jnp.bfloat16)
    total = raw
    for g in range(up_ref.shape[0]):
        inner = jnp.dot(normed, up_ref[g], preferred_element_type=jnp.float32)
        active = jax.nn.gelu(inner).astype(jnp.bfloat16)
        total = total + jnp.dot(active, down_ref[g], preferred_element_type=jnp.float32)
    encoded = total.astype(jnp.bfloat16)
    rows = blocks[0].shape[1]
    keys = jnp.dot(encoded, key_ref[...], preferred_element_type=jnp.float32)
    for h in range(keys.shape[1] // HD):
        cols = slice(h * HD, (h + 1) * HD)
        head = keys[:, cols]
        head = head * lax.rsqrt(jnp.mean(head * head, axis=-1, keepdims=True) + EPSILON)
        keys_ref[:, :, cols] = head.astype(jnp.bfloat16).reshape(GROUP, rows, HD)
    values = jnp.dot(encoded, value_ref[...], preferred_element_type=jnp.float32)
    values_ref[...] = values.astype(jnp.bfloat16).reshape(values_ref.shape)


def encode(slots, blocks, up, down, w_key, w_value):
    count = slots.shape[0]
    _, rows, width = blocks.shape
    columns = w_key.shape[1]
    hidden = up.shape[0] * up.shape[2]

    def whole(array):
        return pl.BlockSpec(array.shape, lambda i, slots_ref, n=array.ndim: (0,) * n)

    block_specs = [
        pl.BlockSpec((1, rows, width), lambda i, slots_ref, j=j: (slots_ref[i * GROUP + j], 0, 0))
        for j in range(GROUP)
    ]
    out_spec = pl.BlockSpec((GROUP, rows, columns), lambda i, slots_ref: (i, 0, 0))
    return pl.pallas_call(
        encode_kernel,
        grid_spec=pltpu.PrefetchScalarGridSpec(
            num_scalar_prefetch=1,
            grid=(count // GROUP,),
            in_specs=block_specs + [whole(a) for a in (up, down, w_key, w_value)],
            out_specs=[out_spec, out_spec],
        ),
        out_shape=[jax.ShapeDtypeStruct((count, rows, columns), jnp.bfloat16)] * 2,
        compiler_params=pltpu.CompilerParams(vmem_limit_bytes=56 * MIB),
        cost_estimate=pl.CostEstimate(
            flops=4 * count * rows * width * (hidden + columns),
            bytes_accessed=2 * (count * rows * (width + 2 * columns) + 2 * width * (hidden + columns)),
            transcendentals=count * rows * hidden,
        ),
    )(slots, *([blocks] * GROUP), up, down, w_key, w_value)


def attend_kernel(parts, queries_ref, *refs):
    keys = jnp.concatenate([r[...].reshape(-1, r.shape[2]) for r in refs[:parts]], axis=0)
    values = jnp.concatenate([r[...].reshape(-1, r.shape[2]) for r in refs[parts : 2 * parts]], axis=0)
    out_ref = refs[2 * parts]
    for h in range(queries_ref.shape[1] // HD):
        cols = slice(h * HD, (h + 1) * HD)
        scores = lax.dot_general(
            queries_ref[:, cols],
            keys[:, cols],
            (((1,), (1,)), ((), ())),
            preferred_element_type=jnp.float32,
        )
        expo = jnp.exp(scores * (LOGIT_SCALE / math.sqrt(HD)))
        weights = (expo / jnp.sum(expo, axis=-1, keepdims=True)).astype(jnp.bfloat16)
        out_ref[:, cols] = jnp.dot(
            weights, values[:, cols], preferred_element_type=jnp.float32
        ).astype(jnp.bfloat16)


def attend(windows, keys, values):
    rows, columns = windows.shape
    parts = len(keys)
    span = pl.BlockSpec((SPAN, columns), lambda i: (i, 0))
    kv = pl.BlockSpec((KN, keys[0].shape[1], columns), lambda i: (i, 0, 0))
    return pl.pallas_call(
        functools.partial(attend_kernel, parts),
        grid=(rows // SPAN,),
        in_specs=[span] + [kv] * (2 * parts),
        out_specs=span,
        out_shape=jax.ShapeDtypeStruct((rows, columns), jnp.bfloat16),
        cost_estimate=pl.CostEstimate(
            flops=4 * rows * KN * NTOK * columns,
            bytes_accessed=4 * rows * columns * (1 + KN * NTOK // SPAN),
            transcendentals=rows * KN * NTOK * columns // HD,
        ),
    )(windows, *keys, *values)


def head_norm(projected):
    shaped = projected.reshape(projected.shape[0], -1, HD)
    scaled = shaped * lax.rsqrt(jnp.mean(shaped * shaped, axis=-1, keepdims=True) + EPSILON)
    return scaled.astype(jnp.bfloat16).reshape(projected.shape)


def gather_pieces(mine):
    dp_count = lax.axis_size("dp")
    column = lax.all_gather(mine, "tensor")
    same_core = [list(range(core, dp_count, 2)) for core in range(2)]
    chip = [[2 * k, 2 * k + 1] for k in range(dp_count // 2)]
    half = lax.all_gather(column, "dp", axis_index_groups=same_core)
    full = lax.all_gather(half, "dp", axis_index_groups=chip)
    full = full.transpose(3, 2, 1, 0, 4, 5)
    return full.reshape(full.shape[:2] + (-1, full.shape[5]))


def own_piece(weight):
    piece = weight.shape[0] // lax.axis_size("dp")
    return lax.dynamic_slice_in_dim(weight, lax.axis_index("dp") * piece, piece, 0)


def gather_weights(w_up, w_down):
    up, down = own_piece(w_up), own_piece(w_down)
    if up.shape == down.shape:
        both = gather_pieces(jnp.stack([up, down]))
        return both[0], both[1]
    return gather_pieces(up[None])[0], gather_pieces(down[None])[0]


def shards(hidden_states, neighbour_ids, database, w_up, w_down, w_query, w_key, w_value):
    dp_count = lax.axis_size("dp")
    shard_blocks = database.shape[0]
    flat_ids = neighbour_ids.reshape(-1)
    request_count = flat_ids.shape[0]
    capacity = max(2, (request_count + dp_count - 1) // dp_count + 1)
    owners = flat_ids // shard_blocks
    local_rows = flat_ids % shard_blocks
    owner_match = (owners[:, None] == jnp.arange(dp_count, dtype=jnp.int32)[None, :]).astype(
        jnp.int32
    )
    positions = jnp.arange(request_count, dtype=jnp.int32)
    earlier = (positions[:, None] > positions[None, :]).astype(jnp.int32)
    ranks = jnp.sum(jnp.dot(earlier, owner_match) * owner_match, axis=1)
    slots = owners * capacity + ranks
    slot_match = slots[None, :] == jnp.arange(dp_count * capacity, dtype=jnp.int32)[:, None]
    requests = jnp.sum(jnp.where(slot_match, local_rows[None, :], 0), axis=1)
    requests = requests.reshape(dp_count, capacity)
    wanted = lax.all_to_all(requests, "dp", split_axis=0, concat_axis=0, tiled=True).reshape(-1)
    up, down = gather_weights(w_up, w_down)
    picked = pick_blocks(wanted, database, PARTS)
    states = lax.all_gather(hidden_states, "tensor", axis=1, tiled=True)
    keys, values = [], []
    for part in picked:
        received = lax.all_to_all(part, "dp", split_axis=0, concat_axis=0, tiled=True)
        part_keys, part_values = encode(slots, received, up, down, w_key, w_value)
        keys.append(part_keys)
        values.append(part_values)
    queries = head_norm(jnp.dot(states, w_query, preferred_element_type=jnp.float32))
    seq_rows, columns = queries.shape
    leading = jnp.zeros((SPAN - 1, columns), jnp.bfloat16)
    windows = jnp.concatenate([queries[SPAN - 1 :], leading], axis=0)
    mixed = attend(windows, keys, values)
    return jnp.concatenate([leading, mixed[: seq_rows - SPAN + 1]], axis=0)


def solution(mesh):
    in_specs = (
        P("dp", "tensor"),
        P("dp", None),
        P("dp", None, None),
        P(None, "tensor"),
        P("tensor", None),
        P(None, "tensor"),
        P(None, "tensor"),
        P(None, "tensor"),
    )
    out_specs = P("dp", "tensor")
    return jax.shard_map(shards, mesh=mesh, in_specs=in_specs, out_specs=out_specs, check_vma=False)
```

time: 504 us -> 398 us (0.79)
  waiting for transfers between devices: 366 us -> 198 us
  Pallas kernels: 0 us -> 131 us
  matrix products: 53.4 us -> 11 us
  other arithmetic: 23.8 us -> 4.87 us
  local copies, waits for them, and re-layouts: 32.5 us -> 21.6 us
    pallas_call x0 -> x4, Pallas kernels: none -> 131 us  [the longest x2 84.6 us: encode(): pl.pallas_call(encode_kernel, grid_spec=pltpu.PrefetchScalarGridSpec(num_...]
    reduce_scatter x1 -> x0, waiting for transfers between devices: 88.3 us -> none  [shards(): lax.psum_scatter(jnp.einsum('btf,fe->bte', active, w_down, preferred_elem...]
    all_to_all x1 -> x2, waiting for transfers between devices: 82.7 us -> 0.01 us  [shards(): lax.all_to_all(part, 'dp', split_axis=0, concat_axis=0, tiled=True)]
    dot_general x6 -> x1, matrix products: 53.3 us -> 10.9 us  [shards(): jnp.dot(states, w_query, preferred_element_type=jnp.float32)]
    convert_element_type x4 -> x1, other arithmetic: 18.9 us -> 1.67 us  [head_norm(): return scaled.astype(jnp.bfloat16).reshape(projected.shape)]
    gather x2 -> x0, local copies, waits for them, and re-layouts: 13.5 us -> none  [the longest x1 7 us: shards(): replies.reshape(dp_count * capacity, block_tokens, enc_width)[slots]]
    slice x2 -> x6, local copies, waits for them, and re-layouts: 0.18 us -> 13.5 us  [the longest x3 12.1 us: gather_weights(): return (both[0], both[1])]
    unnamed x15 -> x9, local copies, waits for them, and re-layouts: 11.3 us -> 2.15 us
  transfers between devices with their start and end apart: 4 -> 6, of which waited for: 4 -> 4; matrix products, arithmetic and copies ran while one was open for 6% -> 8% of each run, Pallas kernels for 0% -> 16%
where the time goes in v1:
time: 398 us; the launch traced here: 397 us
  waiting for transfers between devices  198 us (50%)
  Pallas kernels  131 us (33%)
  local copies, waits for them, and re-layouts  21.6 us (5%)
  between operations  13.2 us (3%)
  matrix products  11 us (3%)
  starting transfers between devices  9.32 us (2%)
  blocking collectives  7.2 us (2%)
  other arithmetic  4.87 us (1%)
    pallas_call x2, Pallas kernels, encode(): pl.pallas_call(encode_kernel, grid_spec=pltpu.PrefetchScalarGridSpec(num_...  84.6 us
    all_gather x1, waiting for transfers between devices, shards(): states = lax.all_gather(hidden_states, 'tensor', axis=1, tiled=True)  82.5 us
    all_gather x1, waiting for transfers between devices, gather_pieces(): half = lax.all_gather(column, 'dp', axis_index_groups=same_core)  71.2 us
    all_gather x1, waiting for transfers between devices, gather_pieces(): column = lax.all_gather(mine, 'tensor')  40.8 us
    pallas_call x1, Pallas kernels, attend(): pl.pallas_call(functools.partial(attend_kernel, parts), grid=(rows // SPA...  27.1 us
    pallas_call x1, Pallas kernels, pick_blocks(): pl.pallas_call(functools.partial(pick_kernel, parts), grid_spec=pltpu.Pre...  19.7 us
    slice x3, local copies, waits for them, and re-layouts, gather_weights(): return (both[0], both[1])  12.1 us
    dot_general x1, matrix products, shards(): jnp.dot(states, w_query, preferred_element_type=jnp.float32)  10.9 us
  transfers between devices with their start and end apart: 6, of which 4 were waited for; matrix products, arithmetic and copies ran while one was open for 8% of the time, Pallas kernels for 16%

profile of v1, /device:TPU:0, one launch (start us, length us, event | category | flops | bytes accessed | tf_op | source)
XLA Modules:
  0.0 397.0 jit_solution(10230421677274458781)
XLA Ops:
  6.5 1.1 dynamic-slice_bitcast_fusion
  7.6 0.8 pad_maximum_fusion
  8.4 0.0 all-gather.10.cloned.1.call-update
  8.4 0.0 all-gather.12.cloned.1.call-start
  8.5 40.8 %all-gather.10.cloned.1.call-done = bf16[8,112,896]{2,1,0:T(8,128)(2,1)} async-done(((bf16[2,112,896]{2,1,0:T(8,128)(2,1)}), bf16[8,112,896]{2,1,0:T(8,128)(2,1)}) %all-gather.10.cloned.1.call-update) | async-done | bytes 1605648 | tf_op jit(solution)/shard_map/all_gather | solution.py:150
  49.3 0.0 all-gather.12.cloned.1.call-update
  49.3 0.0 all-gather.8.cloned.1.call-start
  49.4 0.7 all-gather.8.cloned.1.call-update
  50.0 0.0 all-gather.14.cloned.1.call-start
  50.1 71.2 %all-gather.12.cloned.1.call-done = bf16[16,2,112,896]{3,2,1,0:T(8,128)(2,1)} async-done(((bf16[4,2,112,896]{3,2,1,0:T(8,128)(2,1)}), bf16[16,2,112,896]{3,2,1,0:T(8,128)(2,1)}) %all-gather.12.cloned.1.call-update) | async-done | bytes 6422544 | tf_op jit(solution)/shard_map/all_gather | solution.py:153
  121.3 0.0 all-gather.14.cloned.1.call-update
  121.3 0.7 copy-done
  122.0 0.1 copy.28
  122.0 0.1 reshape.111
  122.1 0.1 fusion.1
  122.3 0.1 select_reduce_fusion
  122.4 0.1 all_to_all.12
  122.5 7.2 %all_to_all.19 = s32[8,1,4]{2,1,0:T(1,128)S(1)} all-to-all(s32[8,1,4]{2,1,0:T(1,128)S(1)} %bitcast.31), channel_id=1, replica_groups=mesh['dp'=8,'tensor'=4] {'dp'}, dimensions={0} | all-to-all | bytes 256 | tf_op jit(solution)/shard_map/all_to_all | solution.py:190
  129.7 0.5 broadcast.125
  130.2 0.7 reduce.3
  130.9 0.6 reshape.112.ids_ref
  131.4 19.7 %shard_map.82 = (bf16[32,64,896]{2,1,0:T(8,128)(2,1)}, bf16[32,64,896]{2,1,0:T(8,128)(2,1)}) custom-call(s32[32]{0:T(128)} %reshape.112.ids_ref, bf16[16,128,896]{2,1,0:T(8,128)(2,1)} %block_ref.1), custom_call_target="tpu_custom_call" | custom-call | bytes 14680064 | tf_op jit(solution)/shard_map/pallas_call | solution.py:33
  151.2 0.0 copy-done.1
  151.2 4.5 %all-to-all-start.2 = ((bf16[32,64,896]{2,1,0:T(8,128)(2,1)}), bf16[32,64,896]{2,1,0:T(8,128)(2,1)}, u32[]{:S(2)}, u32[]{:S(2)}) async-start(bf16[32,64,896]{2,1,0:T(8,128)(2,1)} %get-tuple-element.13), calls=%async_computation.2 | async-start | bytes 7340032 | tf_op jit(solution)/shard_map/all_to_all | solution.py:196
  155.7 82.5 %all-gather.8.cloned.1.call-done = bf16[768,4096]{1,0:T(8,128)(2,1)} async-done(((bf16[768,1024]{1,0:T(8,128)(2,1)}), bf16[768,4096]{1,0:T(8,128)(2,1)}) %all-gather.8.cloned.1.call-update) | async-done | bytes 6291472 | tf_op jit(solution)/shard_map/all_gather | solution.py:193
  238.2 10.9 %convolution_bitcast_fusion = f32[96,8,8,128]{3,1,2,0:T(8,128)S(1)} fusion(bf16[768,4096]{1,0:T(8,128)(2,1)} %all-gather.8.cloned.1.call-done, bf16[4096,1024]{1,0:T(8,128)(2,1)} %param.13), kind=kOutput, calls=%fused_computation.3 | convolution fusion | flops 6442450944 | bytes 17825792 | tf_op jit(solution)/shard_map/dot_general | solution.py:200
  249.1 0.7 copy.32
  249.9 0.9 multiply_reduce_fusion
  250.8 0.7 copy.26
  251.5 0.8 add_rsqrt_fusion
  252.3 0.1 slice.23
  252.3 0.2 copy.34
  252.5 1.7 fusion
  254.2 0.1 pad.4
  254.3 0.4 copy.33
  254.7 1.3 concatenate.6.queries_ref
  256.0 0.0 all-to-all-done.2.refs_0_.refs_1_.refs_2_.refs_3_
  256.0 4.7 %all-to-all-start.1 = ((bf16[32,64,896]{2,1,0:T(8,128)(2,1)}), bf16[32,64,896]{2,1,0:T(8,128)(2,1)}, u32[]{:S(2)}, u32[]{:S(2)}) async-start(bf16[32,64,896]{2,1,0:T(8,128)(2,1)} %get-tuple-element.11), calls=%async_computation.1 | async-start | bytes 7340032 | tf_op jit(solution)/shard_map/all_to_all | solution.py:196
  260.7 3.0 all-gather.14.cloned.1.call-done
  263.7 5.6 %fusion.3 = (bf16[1,4,4,2,112,896]{5,4,0,1,2,3:T(8,128)(2,1)S(1)}, bf16[1,4,4,2,112,896]{5,4,0,1,2,3:T(8,128)(2,1)S(1)}) fusion(bf16[2,4,4,2,112,896]{5,4,0,1,2,3:T(8,128)(2,1)} %bitcast.22), kind=kLoop, calls=%fused_computation.21 | loop fusion | bytes 25690112 | tf_op jit(solution)/shard_map/slice | solution.py:168
  269.3 3.3 copy.30
  272.5 3.2 copy.31
  275.8 42.3 %shard_map.84 = (bf16[24,64,1024]{2,1,0:T(8,128)(2,1)}, bf16[24,64,1024]{2,1,0:T(8,128)(2,1)}) custom-call(s32[24]{0:T(128)} %copy-done.1, bf16[32,64,896]{2,1,0:T(8,128)(2,1)} %all-to-all-done.2.refs_0_.refs_1_.refs_2_.refs_3_, bf16[32,64,896]{2,1,0:T(8,128)(2,1)} %all-to-all-done.2.refs_0_.refs_1_.refs_2_.refs_3_, ...), custom_call_target="tpu_custom_call" | custom-call | flops 25367150592 | bytes 25559040 | tf_op jit(solution)/shard_map/pallas_call | solution.py:86
  318.1 0.0 all-to-all-done.1.refs_0_.refs_1_.refs_2_.refs_3_
  318.1 42.3 %shard_map.83 = (bf16[24,64,1024]{2,1,0:T(8,128)(2,1)}, bf16[24,64,1024]{2,1,0:T(8,128)(2,1)}) custom-call(s32[24]{0:T(128)} %copy-done.1, bf16[32,64,896]{2,1,0:T(8,128)(2,1)} %all-to-all-done.1.refs_0_.refs_1_.refs_2_.refs_3_, bf16[32,64,896]{2,1,0:T(8,128)(2,1)} %all-to-all-done.1.refs_0_.refs_1_.refs_2_.refs_3_, ...), custom_call_target="tpu_custom_call" | custom-call | flops 25367150592 | bytes 25559040 | tf_op jit(solution)/shard_map/pallas_call | solution.py:86
  360.4 27.1 %shard_map.85 = bf16[768,1024]{1,0:T(8,128)(2,1)} custom-call(bf16[768,1024]{1,0:T(8,128)(2,1)} %concatenate.6.queries_ref, bf16[24,64,1024]{2,1,0:T(8,128)(2,1)} %get-tuple-element.12.refs_0_, bf16[24,64,1024]{2,1,0:T(8,128)(2,1)} %get-tuple-element.14.refs_1_, bf16[24,64,1024]{2,1,0:T(8,128)(2,1)} %get-tuple-element.15.refs_2_, ...), custom_call_target="tpu_custom_call" | custom-call | flops 805306368 | bytes 15728640 | tf_op jit(solution)/shard_map/pallas_call | solution.py:128
  387.5 1.4 slice-done
  388.9 1.5 concatenate.7
  (6 shorter events, 0.0 us)
Async XLA Ops:
  6.5 42.8 %all-gather.10.cloned.1.call-start = ((), (), s32[]{:S(2)}) async-start(), calls=%async_computation.4 | async-start | bytes 2007040 | tf_op jit(solution)/shard_map/all_gather | solution.py:150
  8.4 112.9 %all-gather.12.cloned.1.call-start = ((), (), s32[]{:S(2)}) async-start(), calls=%async_computation.5 | async-start | bytes 8028160 | tf_op jit(solution)/shard_map/all_gather | solution.py:153
  49.3 188.9 %all-gather.8.cloned.1.call-start = ((), (), s32[]{:S(2)}) async-start(), calls=%async_computation.3 | async-start | bytes 7864320 | tf_op jit(solution)/shard_map/all_gather | solution.py:193
  50.0 213.6 %all-gather.14.cloned.1.call-start = ((), (), s32[]{:S(2)}) async-start(), calls=%async_computation.6 | async-start | bytes 19267584 | tf_op jit(solution)/shard_map/all_gather | solution.py:154
  121.3 0.7 copy-start
  122.3 28.9 %copy-start.1 = (s32[24]{0:T(128)}, s32[24]{0:T(128)S(1)}, u32[]{:S(2)}) copy-start(s32[24]{0:T(128)S(1)} %multiply_add_fusion.slots_ref) | copy-start | bytes 292
  151.2 104.8 %all-to-all-start.2 = ((bf16[32,64,896]{2,1,0:T(8,128)(2,1)}), bf16[32,64,896]{2,1,0:T(8,128)(2,1)}, u32[]{:S(2)}, u32[]{:S(2)}) async-start(bf16[32,64,896]{2,1,0:T(8,128)(2,1)} %get-tuple-element.13), calls=%async_computation.2 | async-start | bytes 7340032 | tf_op jit(solution)/shard_map/all_to_all | solution.py:196
  256.0 62.1 %all-to-all-start.1 = ((bf16[32,64,896]{2,1,0:T(8,128)(2,1)}), bf16[32,64,896]{2,1,0:T(8,128)(2,1)}, u32[]{:S(2)}, u32[]{:S(2)}) async-start(bf16[32,64,896]{2,1,0:T(8,128)(2,1)} %get-tuple-element.11), calls=%async_computation.1 | async-start | bytes 7340032 | tf_op jit(solution)/shard_map/all_to_all | solution.py:196
  387.5 1.4 slice-start
Sparse Core Ops, SparseCore 0:
  8.9 40.3 all-gather.9
  51.1 70.0 all-gather.11
  122.8 115.3 all-gather.7
  239.6 23.9 all-gather.13

commit v2 on v1

v2 whole, which is shorter than its diff:
```python
import functools
import math

import jax
import jax.numpy as jnp
from jax import lax
from jax.experimental import pallas as pl
from jax.experimental.pallas import tpu as pltpu
from jax.sharding import PartitionSpec as P

HD = 128
SPAN = 64
KN = 2
NTOK = 128

EPSILON = 1e-06
LOGIT_SCALE = 3.0
GROUP = 4
PICK = 4
MIB = 1024 * 1024


def pick_kernel(ids_ref, *refs):
    out_ref = refs[-1]
    for j in range(PICK):
        out_ref[j] = refs[j][0]


def pick_blocks(ids, database):
    count = ids.shape[0]
    _, tokens, width = database.shape
    in_specs = [
        pl.BlockSpec((1, tokens, width), lambda i, ids_ref, j=j: (ids_ref[i * PICK + j], 0, 0))
        for j in range(PICK)
    ]
    return pl.pallas_call(
        pick_kernel,
        grid_spec=pltpu.PrefetchScalarGridSpec(
            num_scalar_prefetch=1,
            grid=(count // PICK,),
            in_specs=in_specs,
            out_specs=pl.BlockSpec((PICK, tokens, width), lambda i, ids_ref: (i, 0, 0)),
        ),
        out_shape=jax.ShapeDtypeStruct((count, tokens, width), database.dtype),
        cost_estimate=pl.CostEstimate(
            flops=0, bytes_accessed=4 * count * tokens * width, transcendentals=0
        ),
    )(ids, *([database] * PICK))


def gelu(x):
    half = 0.5 * x
    root = math.sqrt(2.0 / math.pi)
    return half + half * jnp.tanh(x * (root + (root * 0.044715) * (x * x)))


def encode_kernel(slots_ref, *refs):
    blocks = refs[:GROUP]
    windows_ref, up_ref, down_ref, key_ref, value_ref, out_ref = refs[GROUP:]
    raw = jnp.concatenate([ref[0] for ref in blocks], axis=0).astype(jnp.float32)
    normed = (
        raw * lax.rsqrt(jnp.mean(raw * raw, axis=-1, keepdims=True) + EPSILON)
    ).astype(jnp.bfloat16)
    total = raw
    for g in range(up_ref.shape[0]):
        inner = jnp.dot(normed, up_ref[g], preferred_element_type=jnp.float32)
        active = gelu(inner).astype(jnp.bfloat16)
        total = total + jnp.dot(active, down_ref[g], preferred_element_type=jnp.float32)
    encoded = total.astype(jnp.bfloat16)
    keys = jnp.dot(encoded, key_ref[...], preferred_element_type=jnp.float32)
    values = jnp.dot(encoded, value_ref[...], preferred_element_type=jnp.float32)
    values = values.astype(jnp.bfloat16)
    span_rows = KN * blocks[0].shape[1]
    for h in range(keys.shape[1] // HD):
        cols = slice(h * HD, (h + 1) * HD)
        head = keys[:, cols]
        head = head * lax.rsqrt(jnp.mean(head * head, axis=-1, keepdims=True) + EPSILON)
        head = head.astype(jnp.bfloat16)
        for c in range(GROUP // KN):
            rows = slice(c * span_rows, (c + 1) * span_rows)
            tokens = slice(c * SPAN, (c + 1) * SPAN)
            scores = lax.dot_general(
                windows_ref[tokens, cols],
                head[rows],
                (((1,), (1,)), ((), ())),
                preferred_element_type=jnp.float32,
            )
            expo = jnp.exp(scores * (LOGIT_SCALE / math.sqrt(HD)))
            weights = (expo / jnp.sum(expo, axis=-1, keepdims=True)).astype(jnp.bfloat16)
            out_ref[tokens, cols] = jnp.dot(
                weights, values[rows, cols], preferred_element_type=jnp.float32
            ).astype(jnp.bfloat16)


def encode_and_attend(slots, blocks, windows, up, down, w_key, w_value):
    count = slots.shape[0]
    _, rows, width = blocks.shape
    seq_rows, columns = windows.shape
    hidden = up.shape[0] * up.shape[2]

    def whole(array):
        return pl.BlockSpec(array.shape, lambda i, slots_ref, n=array.ndim: (0,) * n)

    block_specs = [
        pl.BlockSpec((1, rows, width), lambda i, slots_ref, j=j: (slots_ref[i * GROUP + j], 0, 0))
        for j in range(GROUP)
    ]
    window_spec = pl.BlockSpec((GROUP // KN * SPAN, columns), lambda i, slots_ref: (i, 0))
    return pl.pallas_call(
        encode_kernel,
        grid_spec=pltpu.PrefetchScalarGridSpec(
            num_scalar_prefetch=1,
            grid=(count // GROUP,),
            in_specs=block_specs + [window_spec] + [whole(a) for a in (up, down, w_key, w_value)],
            out_specs=window_spec,
        ),
        out_shape=jax.ShapeDtypeStruct((seq_rows, columns), jnp.bfloat16),
        compiler_params=pltpu.CompilerParams(vmem_limit_bytes=60 * MIB),
        cost_estimate=pl.CostEstimate(
            flops=4 * count * rows * width * (hidden + columns),
            bytes_accessed=2 * (count * rows * width + 2 * seq_rows * columns)
            + 4 * width * (hidden + columns),
            transcendentals=count * rows * hidden,
        ),
    )(slots, *([blocks] * GROUP), windows, up, down, w_key, w_value)


def head_norm(projected):
    shaped = projected.reshape(projected.shape[0], -1, HD)
    scaled = shaped * lax.rsqrt(jnp.mean(shaped * shaped, axis=-1, keepdims=True) + EPSILON)
    return scaled.astype(jnp.bfloat16).reshape(projected.shape)


def pass_along(low, high):
    n = lax.axis_size("tensor")
    up = [(i, i + 1) for i in range(n - 1)]
    down = [(i + 1, i) for i in range(n - 1)]
    return lax.ppermute(low, "tensor", up), lax.ppermute(high, "tensor", down)


def project_queries(from_low, from_high, w_query):
    n = lax.axis_size("tensor")
    here = lax.axis_index("tensor")
    depth = from_low[0].shape[1]
    projected = 0.0
    for m in range(n):
        shard = from_low[0]
        if m:
            shard = jnp.where(here + m < n, from_high[m], from_low[n - m])
        rows = lax.dynamic_slice_in_dim(w_query, (here + m) % n * depth, depth, 0)
        projected = projected + jnp.dot(shard, rows, preferred_element_type=jnp.float32)
    return head_norm(projected)


def gather_pieces(mine):
    return lax.all_gather(mine, "tensor")


def gather_cores(column):
    same_core = [list(range(core, lax.axis_size("dp"), 2)) for core in range(2)]
    return lax.all_gather(column, "dp", axis_index_groups=same_core)


def gather_chip(half):
    chip = [[2 * k, 2 * k + 1] for k in range(lax.axis_size("dp") // 2)]
    full = lax.all_gather(half, "dp", axis_index_groups=chip)
    full = full.transpose(3, 2, 1, 0, 4, 5)
    return full.reshape(full.shape[:2] + (-1, full.shape[5]))


def own_piece(weight):
    piece = weight.shape[0] // lax.axis_size("dp")
    return lax.dynamic_slice_in_dim(weight, lax.axis_index("dp") * piece, piece, 0)


def gather_columns(w_up, w_down):
    up, down = own_piece(w_up), own_piece(w_down)
    if up.shape == down.shape:
        return [gather_pieces(jnp.stack([up, down]))]
    return [gather_pieces(up[None]), gather_pieces(down[None])]


def shards(hidden_states, neighbour_ids, database, w_up, w_down, w_query, w_key, w_value):
    dp_count = lax.axis_size("dp")
    shard_blocks = database.shape[0]
    flat_ids = neighbour_ids.reshape(-1)
    request_count = flat_ids.shape[0]
    capacity = max(2, (request_count + dp_count - 1) // dp_count + 1)
    owners = flat_ids // shard_blocks
    local_rows = flat_ids % shard_blocks
    owner_match = (owners[:, None] == jnp.arange(dp_count, dtype=jnp.int32)[None, :]).astype(
        jnp.int32
    )
    positions = jnp.arange(request_count, dtype=jnp.int32)
    earlier = (positions[:, None] > positions[None, :]).astype(jnp.int32)
    ranks = jnp.sum(jnp.dot(earlier, owner_match) * owner_match, axis=1)
    slots = owners * capacity + ranks
    slot_match = slots[None, :] == jnp.arange(dp_count * capacity, dtype=jnp.int32)[:, None]
    requests = jnp.sum(jnp.where(slot_match, local_rows[None, :], 0), axis=1)
    requests = requests.reshape(dp_count, capacity)
    wanted = lax.all_to_all(requests, "dp", split_axis=0, concat_axis=0, tiled=True).reshape(-1)
    picked = pick_blocks(wanted, database)
    columns = gather_columns(w_up, w_down)
    first = pass_along(hidden_states, hidden_states)
    picked, columns, first = lax.optimization_barrier((picked, columns, first))
    received = lax.all_to_all(picked, "dp", split_axis=0, concat_axis=0, tiled=True)
    from_low, from_high = [hidden_states, first[0]], [hidden_states, first[1]]
    for _ in range(2, lax.axis_size("tensor")):
        low, high = pass_along(from_low[-1], from_high[-1])
        from_low.append(low)
        from_high.append(high)
    halves = [gather_cores(column) for column in columns]
    halves, received, from_low, from_high = lax.optimization_barrier(
        (halves, received, from_low, from_high)
    )
    up, down = [weight for half in halves for weight in gather_chip(half)]
    queries = project_queries(from_low, from_high, w_query)
    seq_rows = queries.shape[0]
    leading = jnp.zeros((SPAN - 1, queries.shape[1]), jnp.bfloat16)
    windows = jnp.concatenate([queries[SPAN - 1 :], leading], axis=0)
    mixed = encode_and_attend(slots, received, windows, up, down, w_key, w_value)
    return jnp.concatenate([leading, mixed[: seq_rows - SPAN + 1]], axis=0)


def solution(mesh):
    in_specs = (
        P("dp", "tensor"),
        P("dp", None),
        P("dp", None, None),
        P(None, "tensor"),
        P("tensor", None),
        P(None, "tensor"),
        P(None, "tensor"),
        P(None, "tensor"),
    )
    out_specs = P("dp", "tensor")
    return jax.shard_map(shards, mesh=mesh, in_specs=in_specs, out_specs=out_specs, check_vma=False)
```

time: 398 us -> 360 us (0.905)
  waiting for transfers between devices: 198 us -> 171 us
  Pallas kernels: 131 us -> 105 us
  starting transfers between devices: 9.32 us -> 22 us
    all_gather x4 -> x3, waiting for transfers between devices: 198 us -> 9.09 us  [the longest x1 6.65 us: gather_chip(): full = lax.all_gather(half, 'dp', axis_index_groups=chip)]
    ppermute x0 -> x6, waiting for transfers between devices: none -> 110 us  [pass_along(): return (lax.ppermute(low, 'tensor', up), lax.ppermute(high, 'tensor', down))]
    all_to_all x2 -> x1, waiting for transfers between devices: 0.01 us -> 51.7 us  [shards(): lax.all_to_all(picked, 'dp', split_axis=0, concat_axis=0, tiled=True)]
    pallas_call x4 -> x2, Pallas kernels: 131 us -> 105 us  [the longest x1 96.3 us: encode_and_attend(): pl.pallas_call(encode_kernel, grid_spec=pltpu.PrefetchScalarGridSpec(num_...]
    ppermute x0 -> x6, starting transfers between devices: none -> 17 us  [pass_along(): return (lax.ppermute(low, 'tensor', up), lax.ppermute(high, 'tensor', down))]
    slice x3 -> x0, local copies, waits for them, and re-layouts: 12.1 us -> none  [gather_weights(): return (both[0], both[1])]
    another operation x1 -> x4, local copies, waits for them, and re-layouts: 1.06 us -> 13.1 us  [the longest x3 12.1 us: shards(): up, down = [weight for half in halves for weight in gather_chip(half)]]
    all_to_all x2 -> x1, starting transfers between devices: 9.2 us -> 4.85 us  [shards(): lax.all_to_all(picked, 'dp', split_axis=0, concat_axis=0, tiled=True)]
  transfers between devices with their start and end apart: 6 -> 10, of which waited for: 4 -> 8; matrix products, arithmetic and copies ran while one was open for 8% -> 6% of each run, Pallas kernels for 16% -> 2%
where the time goes in v2:
time: 360 us
  waiting for transfers between devices  171 us (48%)
  Pallas kernels  105 us (29%)
  local copies, waits for them, and re-layouts  23.9 us (7%)
  starting transfers between devices  22 us (6%)
  between operations  13.4 us (4%)
  matrix products  11.5 us (3%)
  blocking collectives  8.17 us (2%)
  other arithmetic  4.85 us (1%)
    ppermute x6, waiting for transfers between devices, pass_along(): return (lax.ppermute(low, 'tensor', up), lax.ppermute(high, 'tensor', down))  110 us
    pallas_call x1, Pallas kernels, encode_and_attend(): pl.pallas_call(encode_kernel, grid_spec=pltpu.PrefetchScalarGridSpec(num_...  96.3 us
    all_to_all x1, waiting for transfers between devices, shards(): lax.all_to_all(picked, 'dp', split_axis=0, concat_axis=0, tiled=True)  51.7 us
    ppermute x6, starting transfers between devices, pass_along(): return (lax.ppermute(low, 'tensor', up), lax.ppermute(high, 'tensor', down))  17 us
    another operation x3, local copies, waits for them, and re-layouts, shards(): up, down = [weight for half in halves for weight in gather_chip(half)]  12.1 us
    dot_general x4, matrix products, project_queries(): jnp.dot(shard, rows, preferred_element_type=jnp.float32)  11.3 us
    pallas_call x1, Pallas kernels, pick_blocks(): pl.pallas_call(pick_kernel, grid_spec=pltpu.PrefetchScalarGridSpec(num_sc...  8.99 us
    all_to_all x1, blocking collectives, shards(): lax.all_to_all(requests, 'dp', split_axis=0, concat_axis=0, tiled=True)  8.17 us
  transfers between devices with their start and end apart: 10, of which 8 were waited for; matrix products, arithmetic and copies ran while one was open for 6% of the time, Pallas kernels for 2%

profile of v2, /device:TPU:0, one launch (start us, length us, event | category | flops | bytes accessed | tf_op | source)
XLA Modules:
  0.0 359.7 jit_solution(10537297906572775745)
XLA Ops:
  6.5 1.1 dynamic-slice_bitcast_fusion
  7.6 0.8 pad_maximum_fusion
  8.5 5.0 %collective-permute-start = (bf16[768,1024]{1,0:T(8,128)(2,1)}, bf16[768,1024]{1,0:T(8,128)(2,1)S(1)}, u32[]{:S(2)}, u32[]{:S(2)}) collective-permute-start(bf16[768,1024]{1,0:T(8,128)(2,1)} %param.8), channel_id=1, source_target_pairs={{0,1},{1,2},{2,3},{4,5},{5,6},{6,7},{8,9},{9,10},{10,11},{12,13},{... | collective-permute-start | bytes 4718600 | tf_op jit(solution)/shard_map/ppermute | solution.py:138
  13.5 1.3 collective-permute-start.1
  14.8 0.8 copy.26
  15.7 0.1 fusion.19
  15.8 0.1 select_reduce_fusion
  15.9 0.1 all_to_all.9
  16.0 8.2 %all_to_all.14 = s32[8,1,4]{2,1,0:T(1,128)S(1)} all-to-all(s32[8,1,4]{2,1,0:T(1,128)S(1)} %bitcast.30), channel_id=1, replica_groups=mesh['dp'=8,'tensor'=4] {'dp'}, dimensions={0} | all-to-all | bytes 256 | tf_op jit(solution)/shard_map/all_to_all | solution.py:201
  24.2 0.6 broadcast.133
  24.8 0.6 reduce.3
  25.4 0.6 reshape.111.ids_ref
  26.0 9.0 %shard_map.82 = bf16[32,128,896]{2,1,0:T(8,128)(2,1)} custom-call(s32[32]{0:T(128)} %reshape.111.ids_ref, bf16[16,128,896]{2,1,0:T(8,128)(2,1)} %refs_3_.1, bf16[16,128,896]{2,1,0:T(8,128)(2,1)} %refs_3_.1, bf16[16,128,896]{2,1,0:T(8,128)(2,1)} %refs_3_.1, bf16[16,128,896]{2,1,0:T(8,128)(2,1)} %refs_3_.1), custom_call_target="tpu_custom_call" | custom-call | bytes 14680064 | tf_op jit(solution)/shard_map/pallas_call | solution.py:36
  35.0 38.2 %collective-permute-done = bf16[768,1024]{1,0:T(8,128)(2,1)S(1)} collective-permute-done((bf16[768,1024]{1,0:T(8,128)(2,1)}, bf16[768,1024]{1,0:T(8,128)(2,1)S(1)}, u32[]{:S(2)}, u32[]{:S(2)}) %collective-permute-start) | collective-permute-done | bytes 1572896 | tf_op jit(solution)/shard_map/ppermute | solution.py:138
  73.2 4.1 %collective-permute-done.1 = bf16[768,1024]{1,0:T(8,128)(2,1)S(1)} collective-permute-done((bf16[768,1024]{1,0:T(8,128)(2,1)}, bf16[768,1024]{1,0:T(8,128)(2,1)S(1)}, u32[]{:S(2)}, u32[]{:S(2)}) %collective-permute-start.1) | collective-permute-done | bytes 1572896 | tf_op jit(solution)/shard_map/ppermute | solution.py:138
  77.3 4.9 %all-to-all-start.1 = ((bf16[32,128,896]{2,1,0:T(8,128)(2,1)}), bf16[32,128,896]{2,1,0:T(8,128)(2,1)}, u32[]{:S(2)}, u32[]{:S(2)}) async-start(bf16[32,128,896]{2,1,0:T(8,128)(2,1)} %shard_map.82), calls=%async_computation.1 | async-start | bytes 14680064 | tf_op jit(solution)/shard_map/all_to_all | solution.py:206
  82.2 3.5 collective-permute-start.2
  85.7 1.3 collective-permute-start.4
  87.0 32.7 %collective-permute-done.2 = bf16[768,1024]{1,0:T(8,128)(2,1)S(1)} collective-permute-done((bf16[768,1024]{1,0:T(8,128)(2,1)S(1)}, bf16[768,1024]{1,0:T(8,128)(2,1)S(1)}, u32[]{:S(2)}, u32[]{:S(2)}) %collective-permute-start.2) | collective-permute-done | bytes 1572896 | tf_op jit(solution)/shard_map/ppermute | solution.py:138
  119.7 4.5 %collective-permute-start.3 = (bf16[768,1024]{1,0:T(8,128)(2,1)S(1)}, bf16[768,1024]{1,0:T(8,128)(2,1)S(1)}, u32[]{:S(2)}, u32[]{:S(2)}) collective-permute-start(bf16[768,1024]{1,0:T(8,128)(2,1)S(1)} %collective-permute-done.2), channel_id=1, source_target_pairs={{0,1},{1,2},{2,3},{4,5},{5,6},{6,7},{8,9},{9,10},{10,11},{12,13},{... | collective-permute-start | bytes 4718600 | tf_op jit(solution)/shard_map/ppermute | solution.py:138
  124.2 1.5 collective-permute-start.5
  125.7 31.8 %collective-permute-done.3 = bf16[768,1024]{1,0:T(8,128)(2,1)S(1)} collective-permute-done((bf16[768,1024]{1,0:T(8,128)(2,1)S(1)}, bf16[768,1024]{1,0:T(8,128)(2,1)S(1)}, u32[]{:S(2)}, u32[]{:S(2)}) %collective-permute-start.3) | collective-permute-done | bytes 1572896 | tf_op jit(solution)/shard_map/ppermute | solution.py:138
  157.5 1.2 copy-done.6
  158.8 3.0 collective-permute-done.5
  161.8 51.7 %all-to-all-done.1.refs_0_.refs_1_.refs_2_.refs_3_ = bf16[32,128,896]{2,1,0:T(8,128)(2,1)} async-done(((bf16[32,128,896]{2,1,0:T(8,128)(2,1)}), bf16[32,128,896]{2,1,0:T(8,128)(2,1)}, u32[]{:S(2)}, u32[]{:S(2)}) %all-to-all-start.1) | async-done | bytes 7340064 | tf_op jit(solution)/shard_map/all_to_all | solution.py:206
  213.4 2.4 all-gather.9.cloned.1.call-done
  216.0 4.0 %fusion.7 = f32[768,1024]{1,0:T(8,128)S(1)} fusion(bf16[768,1024]{1,0:T(8,128)(2,1)} %param.8, bf16[4096,1024]{1,0:T(8,128)(2,1)} %param.13, s32[]{:T(128)S(6)} %select_n.87), kind=kOutput, calls=%fused_computation.10 | convolution fusion | flops 1610612736 | bytes 6815748 | tf_op jit(solution)/shard_map/dot_general | solution.py:151
  220.1 3.6 fusion.3
  223.7 0.2 copy-done.1
  223.9 0.7 copy-done.7
  224.6 1.8 fusion.5
  226.4 1.9 add_bitcast_fusion
  228.4 0.7 copy.32
  229.1 0.9 multiply_reduce_fusion
  230.0 0.7 copy.28
  230.7 0.8 add_rsqrt_fusion
  231.6 0.2 copy.34
  231.7 1.7 fusion
  233.4 0.1 pad.4
  233.5 0.4 copy.33
  233.9 1.3 concatenate.6.refs_4_
  235.2 6.6 %all-gather.11.cloned.1.call-done = bf16[8,4,2,112,896]{4,3,2,1,0:T(8,128)(2,1)} async-done(((bf16[4,4,2,112,896]{4,3,2,1,0:T(8,128)(2,1)}), bf16[8,4,2,112,896]{4,3,2,1,0:T(8,128)(2,1)}) %all-gather.11.cloned.1.call-update) | async-done | bytes 12845072 | tf_op jit(solution)/shard_map/all_gather | solution.py:166
  241.9 5.6 %fusion.25 = (bf16[1,4,4,2,112,896]{5,4,0,1,2,3:T(8,128)(2,1)S(1)}, bf16[1,4,4,2,112,896]{5,4,0,1,2,3:T(8,128)(2,1)S(1)}) fusion(bf16[2,4,4,2,112,896]{5,4,0,1,2,3:T(8,128)(2,1)} %bitcast.21), kind=kLoop, calls=%fused_computation.39 | loop fusion | bytes 25690112 | tf_op jit(solution)/shard_map/unstack | solution.py:216
  247.4 3.3 copy.30
  250.7 3.3 copy.31
  254.0 96.3 %shard_map.83 = bf16[768,1024]{1,0:T(8,128)(2,1)} custom-call(s32[24]{0:T(128)} %copy-done.8, bf16[32,128,896]{2,1,0:T(8,128)(2,1)} %all-to-all-done.1.refs_0_.refs_1_.refs_2_.refs_3_, bf16[32,128,896]{2,1,0:T(8,128)(2,1)} %all-to-all-done.1.refs_0_.refs_1_.refs_2_.refs_3_, bf16[32,128,896]{2,1,0:T(8,128)(2,1)} %all-to-all-done.1.refs_0_.refs_1_.refs_2_.refs_3_, ...), custom_call_target="tpu_custom_call" | custom-call | flops 50734301184 | bytes 25165824 | tf_op jit(solution)/shard_map/pallas_call | solution.py:109
  350.2 1.4 slice-done
  351.6 1.5 concatenate.7
  (33 shorter events, 0.4 us)
Async XLA Ops:
  6.5 70.7 %all-gather.7.cloned.1.call-start = ((), (), s32[]{:S(2)}) async-start(), calls=%async_computation.2 | async-start | bytes 2007040 | tf_op jit(solution)/shard_map/all_gather | solution.py:156
  8.4 207.5 %all-gather.9.cloned.1.call-start = ((), (), s32[]{:S(2)}) async-start(), calls=%async_computation.3 | async-start | bytes 8028160 | tf_op jit(solution)/shard_map/all_gather | solution.py:161
  8.5 64.7 %collective-permute-start = (bf16[768,1024]{1,0:T(8,128)(2,1)}, bf16[768,1024]{1,0:T(8,128)(2,1)S(1)}, u32[]{:S(2)}, u32[]{:S(2)}) collective-permute-start(bf16[768,1024]{1,0:T(8,128)(2,1)} %param.8), channel_id=1, source_target_pairs={{0,1},{1,2},{2,3},{4,5},{5,6},{6,7},{8,9},{9,10},{10,11},{12,13},{... | collective-permute-start | bytes 4718600 | tf_op jit(solution)/shard_map/ppermute | solution.py:138
  13.5 63.8 %collective-permute-start.1 = (bf16[768,1024]{1,0:T(8,128)(2,1)}, bf16[768,1024]{1,0:T(8,128)(2,1)S(1)}, u32[]{:S(2)}, u32[]{:S(2)}) collective-permute-start(bf16[768,1024]{1,0:T(8,128)(2,1)} %param.8), channel_id=1, source_target_pairs={{1,0},{2,1},{3,2},{5,4},{6,5},{7,6},{9,8},{10,9},{11,10},{13,12},{... | collective-permute-start | bytes 4718600 | tf_op jit(solution)/shard_map/ppermute | solution.py:138
  15.8 19.2 %copy-start.8 = (s32[24]{0:T(128)}, s32[24]{0:T(128)S(1)}, u32[]{:S(2)}) copy-start(s32[24]{0:T(128)S(1)} %multiply_add_fusion.slots_ref) | copy-start | bytes 292
  77.3 8.4 %copy-start = (bf16[768,1024]{1,0:T(8,128)(2,1)}, bf16[768,1024]{1,0:T(8,128)(2,1)S(1)}, u32[]{:S(2)}) copy-start(bf16[768,1024]{1,0:T(8,128)(2,1)S(1)} %collective-permute-done.1) | copy-start | bytes 4718596
  77.3 136.1 %all-to-all-start.1 = ((bf16[32,128,896]{2,1,0:T(8,128)(2,1)}), bf16[32,128,896]{2,1,0:T(8,128)(2,1)}, u32[]{:S(2)}, u32[]{:S(2)}) async-start(bf16[32,128,896]{2,1,0:T(8,128)(2,1)} %shard_map.82), calls=%async_computation.1 | async-start | bytes 14680064 | tf_op jit(solution)/shard_map/all_to_all | solution.py:206
  82.2 159.7 %all-gather.11.cloned.1.call-start = ((), (), s32[]{:S(2)}) async-start(), calls=%async_computation.4 | async-start | bytes 19267584 | tf_op jit(solution)/shard_map/all_gather | solution.py:166
  82.2 37.5 %collective-permute-start.2 = (bf16[768,1024]{1,0:T(8,128)(2,1)S(1)}, bf16[768,1024]{1,0:T(8,128)(2,1)S(1)}, u32[]{:S(2)}, u32[]{:S(2)}) collective-permute-start(bf16[768,1024]{1,0:T(8,128)(2,1)S(1)} %collective-permute-done), channel_id=1, source_target_pairs={{0,1},{1,2},{2,3},{4,5},{5,6},{6,7},{8,9},{9,10},{10,11},{12,13},{... | collective-permute-start | bytes 4718600 | tf_op jit(solution)/shard_map/ppermute | solution.py:138
  85.7 38.5 %collective-permute-start.4 = (bf16[768,1024]{1,0:T(8,128)(2,1)S(1)}, bf16[768,1024]{1,0:T(8,128)(2,1)S(1)}, u32[]{:S(2)}, u32[]{:S(2)}) collective-permute-start(bf16[768,1024]{1,0:T(8,128)(2,1)S(1)} %collective-permute-done.1), channel_id=1, source_target_pairs={{1,0},{2,1},{3,2},{5,4},{6,5},{7,6},{9,8},{10,9},{11,10},{13,12},{... | collective-permute-start | bytes 4718600 | tf_op jit(solution)/shard_map/ppermute | solution.py:138
  119.7 6.0 %copy-start.2 = (bf16[768,1024]{1,0:T(8,128)(2,1)}, bf16[768,1024]{1,0:T(8,128)(2,1)S(1)}, u32[]{:S(2)}) copy-start(bf16[768,1024]{1,0:T(8,128)(2,1)S(1)} %collective-permute-done.2) | copy-start | bytes 4718596
  119.7 37.8 %collective-permute-start.3 = (bf16[768,1024]{1,0:T(8,128)(2,1)S(1)}, bf16[768,1024]{1,0:T(8,128)(2,1)S(1)}, u32[]{:S(2)}, u32[]{:S(2)}) collective-permute-start(bf16[768,1024]{1,0:T(8,128)(2,1)S(1)} %collective-permute-done.2), channel_id=1, source_target_pairs={{0,1},{1,2},{2,3},{4,5},{5,6},{6,7},{8,9},{9,10},{10,11},{12,13},{... | collective-permute-start | bytes 4718600 | tf_op jit(solution)/shard_map/ppermute | solution.py:138
  124.2 33.3 %copy-start.4 = (bf16[768,1024]{1,0:T(8,128)(2,1)}, bf16[768,1024]{1,0:T(8,128)(2,1)S(1)}, u32[]{:S(2)}) copy-start(bf16[768,1024]{1,0:T(8,128)(2,1)S(1)} %collective-permute-done.4) | copy-start | bytes 4718596
  124.2 37.5 %collective-permute-start.5 = (bf16[768,1024]{1,0:T(8,128)(2,1)S(1)}, bf16[768,1024]{1,0:T(8,128)(2,1)S(1)}, u32[]{:S(2)}, u32[]{:S(2)}) collective-permute-start(bf16[768,1024]{1,0:T(8,128)(2,1)S(1)} %collective-permute-done.4), channel_id=1, source_target_pairs={{1,0},{2,1},{3,2},{5,4},{6,5},{7,6},{9,8},{10,9},{11,10},{13,12},{... | collective-permute-start | bytes 4718600 | tf_op jit(solution)/shard_map/ppermute | solution.py:138
  157.5 1.2 copy-start.6
  216.0 4.0 %copy-start.3 = (bf16[768,1024]{1,0:T(8,128)(2,1)S(1)}, bf16[768,1024]{1,0:T(8,128)(2,1)}, u32[]{:S(2)}) copy-start(bf16[768,1024]{1,0:T(8,128)(2,1)} %copy-done.2) | copy-start | bytes 4718596
  216.0 4.0 %copy-start.5 = (bf16[768,1024]{1,0:T(8,128)(2,1)S(1)}, bf16[768,1024]{1,0:T(8,128)(2,1)}, u32[]{:S(2)}) copy-start(bf16[768,1024]{1,0:T(8,128)(2,1)} %copy-done.4) | copy-start | bytes 4718596
  216.0 7.7 %slice-start.1 = ((s8[8388608]{0:T(1024)(128)(4,1)}), s8[4194304]{0:T(1024)(128)(4,1)S(1)}, s32[]{:S(2)}) async-start(s8[8388608]{0:T(1024)(128)(4,1)} %bitcast.28), calls=%async_computation.6 | async-start | bytes 8388608
  220.0 3.6 %slice-start.2 = ((s8[8388608]{0:T(1024)(128)(4,1)}), s8[4194304]{0:T(1024)(128)(4,1)S(1)}, s32[]{:S(2)}) async-start(s8[8388608]{0:T(1024)(128)(4,1)} %bitcast.28), calls=%async_computation.7 | async-start | bytes 8388608
  220.0 3.8 %copy-start.1 = (bf16[768,1024]{1,0:T(8,128)(2,1)S(1)}, bf16[768,1024]{1,0:T(8,128)(2,1)}, u32[]{:S(2)}) copy-start(bf16[768,1024]{1,0:T(8,128)(2,1)} %copy-done) | copy-start | bytes 4718596
  220.1 4.6 %copy-start.7 = (bf16[768,1024]{1,0:T(8,128)(2,1)S(1)}, bf16[768,1024]{1,0:T(8,128)(2,1)}, u32[]{:S(2)}) copy-start(bf16[768,1024]{1,0:T(8,128)(2,1)} %copy-done.6) | copy-start | bytes 4718596
  350.2 1.4 slice-start
Sparse Core Ops, SparseCore 0:
  8.9 62.6 all-gather.6
  77.4 138.4 all-gather.8
  217.4 24.3 all-gather.10
